TPU v7x, 32 devices: a whole 2x2x4 slice. The times are simulated.
32 devices in a mesh: rep: 2 (over y), dp: 4 (over z), mp: 2 (over x), sub: 2 (over core).
Axes of the slice: x: 2, y: 2, z: 4, core: 2. Of those that a mesh axis runs over, the one named last changes fastest.
Arguments:
- activations: bfloat16 [2048, 2048], P(('rep', 'dp')), parts along dimension 0, may hold values from -6 to 6
- cotangent: bfloat16 [2048, 2, 512], P(('rep', 'dp'), 'mp', 'sub'), parts along dimension 0, may hold values from -6 to 6
- owner_table: int32 [4, 4], P(('rep', 'mp')), parts along dimension 0, may hold values from 0 to 3, each once within a row
Outputs:
- update: bfloat16 [16, 512, 512], P(('rep', 'mp'), 'dp', 'sub'), parts along dimension 0
There are 2 independent parts, one for each index of `rep`. A program takes and returns all parts, laid end to end along the dimension named above; each array names one. Nothing has to cross between parts.
Inputs may be any that keep to these rules, and one draw needn't show every extreme that they name: Each row of owner_table names every block number of its layer group exactly once.
All inputs are finite; a program needn't handle non-finite values.
Results may differ from a plain program's by a relative error of at most 0.015.
Values may be sent and summed in bfloat16 or wider, within the bound.
A program may use at most 64 MiB of HBM per device.

v0:
```python
import math

import jax
import jax.numpy as jnp
from jax import lax
from jax.sharding import PartitionSpec as P

D = 2048
B = 512
ITERS = 2


damping_rel = 0.05


def from_partner(x, axis, distance):
    return lax.ppermute(x, axis, [(i, i ^ 1 << distance) for i in range(lax.axis_size(axis))])


def matmul_high(left_mat, right_mat):
    return jnp.dot(left_mat, right_mat, precision=lax.Precision.HIGHEST)


def newton_root(statistic):
    identity = jnp.eye(statistic.shape[0], dtype=statistic.dtype)
    damped = statistic + damping_rel * (jnp.trace(statistic) / statistic.shape[0]) * identity
    frob = jnp.sqrt(jnp.sum(damped * damped))
    scale_init = 2.5 / frob
    root_now = scale_init**0.25 * identity
    coupled = scale_init * damped
    for sweep in range(ITERS):
        factor = (5.0 * identity - coupled) * 0.25
        root_now = matmul_high(root_now, factor)
        squared = matmul_high(factor, factor)
        fourth = matmul_high(squared, squared)
        coupled = matmul_high(fourth, coupled)
    return root_now


def shards(activations, cotangent, owner_table):
    table_row = owner_table[0]
    col_count = cotangent.shape[1]
    half_cols = cotangent.shape[2]
    act_blocks = activations.reshape(activations.shape[0], D // B, B)
    row_blocks = table_row // col_count
    col_blocks = table_row % col_count
    act_sel = jnp.take(act_blocks, row_blocks, axis=1)
    cot_sel = jnp.take(cotangent, col_blocks, axis=1)
    own_half = lax.psum_scatter(
        jnp.einsum("tkb,tkh->kbh", act_sel, cot_sel, preferred_element_type=jnp.float32).astype(
            jnp.bfloat16
        ),
        "dp",
        scatter_dimension=0,
        tiled=True,
    ).astype(jnp.float32)[0]
    peer_half = from_partner(own_half.astype(jnp.bfloat16), "sub", 0).astype(own_half.dtype)
    sub_index = lax.axis_index("sub")
    first_core = sub_index == 0
    whole_grad = jnp.where(
        first_core,
        jnp.concatenate([own_half, peer_half], axis=1),
        jnp.concatenate([peer_half, own_half], axis=1),
    )
    factor_side = jnp.where(first_core, whole_grad, whole_grad.T)
    root_own = newton_root(matmul_high(factor_side, factor_side.T)).astype(jnp.bfloat16)
    root_peer = from_partner(root_own, "sub", 0)
    left_b = jnp.where(first_core, root_own, root_peer)
    right_b = jnp.where(first_core, root_peer, root_own)
    right_cols = lax.dynamic_slice_in_dim(right_b, sub_index * half_cols, half_cols, 1)
    grad_b = whole_grad.astype(jnp.bfloat16)
    carried = jnp.dot(grad_b, right_cols, preferred_element_type=jnp.float32).astype(jnp.bfloat16)
    block_update = (
        jnp.dot(left_b, carried, preferred_element_type=jnp.float32) * math.sqrt(B)
    ).astype(jnp.bfloat16)
    received = lax.all_to_all(block_update[None], "dp", split_axis=1, concat_axis=0, tiled=True)
    return received


def solution(mesh):
    in_specs = (P(("rep", "dp"), None), P(("rep", "dp"), "mp", "sub"), P(("rep", "mp"), None))
    out_specs = P(("rep", "mp"), "dp", "sub")
    return jax.shard_map(shards, mesh=mesh, in_specs=in_specs, out_specs=out_specs, check_vma=False)
```

profile of v0, /device:TPU:0, one launch (start us, length us, event | category | flops | bytes accessed | tf_op | source)
XLA Modules:
  0.0 85.7 jit_solution(14885833921843418054)
XLA Ops:
  6.5 0.7 fusion.35
  7.2 0.7 compare_and_fusion
  7.9 1.5 %copy.16 = bf16[256,2048]{0,1:T(8,128)(2,1)S(1)} copy(bf16[256,2048]{1,0:T(8,128)(2,1)} %param.3) | data formatting | bytes 2097152 | tf_op args[0]
  9.4 0.5 copy.17
  9.9 0.6 gather_fusion
  10.6 1.6 %convolution_convert_fusion = bf16[4,512,256]{2,1,0:T(8,128)(2,1)} fusion(bf16[4,256,512]{2,1,0:T(8,128)(2,1)S(1)} %gather_fusion, pred[4]{0:T(512)(128)(4,1)S(1)} %compare_and_fusion, bf16[256,256]{1,0:T(8,128)(2,1)S(1)} %bitcast.30), kind=kOutput, calls=%fused_computation.1 | convolution fusion | flops 269484032 | bytes 2228228 | tf_op jit(solution)/shard_map/tkb,tkh->kbh/dot_general | solution.py:50
  12.2 30.0 %reduce-scatter.2.cloned.1.call-done = bf16[1,512,256]{2,1,0:T(8,128)(2,1)} async-done(((bf16[4,512,256]{2,1,0:T(8,128)(2,1)}), bf16[1,512,256]{2,1,0:T(8,128)(2,1)}) %reduce-scatter.2.cloned.1.call-update) | async-done | bytes 262160 | tf_op jit(solution)/shard_map/reduce_scatter | solution.py:49
  42.2 1.0 %bitcast_convert_fusion = f32[512,256]{1,0:T(8,128)S(1)} fusion(bf16[1,512,256]{2,1,0:T(8,128)(2,1)} %reduce-scatter.2.cloned.1.call-done), kind=kLoop, calls=%fused_computation.50 | loop fusion | flops 131072 | bytes 786432 | tf_op jit(solution)/shard_map/squeeze | solution.py:49
  43.2 0.8 collective-permute-done
  44.1 0.3 copy.19
  44.5 2.6 %select_reduce_fusion = (f32[]{:T(128)}, f32[512,512]{1,0:T(8,128)S(1)}) fusion(f32[512,512]{0,1:T(8,128)S(1)} %copy.19, pred[]{:T(512)S(6)} %eq.18, f32[512,256]{1,0:T(8,128)S(1)} %bitcast_convert_fusion, f32[512,256]{1,0:T(8,128)S(1)} %convert_element_type.22), kind=kOutput, calls=%fused_computation.20 | convolution fusion | flops 1612447744 | bytes 3145733 | tf_op jit(solution)/shard_map/dot_general | solution.py:21
  47.7 0.9 %multiply_reduce_fusion = f32[]{:T(128)} fusion(f32[512,512]{1,0:T(8,128)S(1)} %get-tuple-element.6, f32[]{:T(128)S(6)} %mul_shard_map.3), kind=kLoop, calls=%fused_computation.18 | loop fusion | flops 1310719 | bytes 1048584 | tf_op jit(solution)/shard_map/reduce_sum | solution.py:27
  49.3 2.0 %fusion.11 = f32[512,512]{1,0:T(8,128)S(1)} fusion(f32[]{:T(128)S(6)} %div.8, f32[512,512]{1,0:T(8,128)S(1)} %get-tuple-element.6, f32[]{:T(128)S(6)} %mul_shard_map.3), kind=kOutput, calls=%fused_computation.24 | convolution fusion | flops 1612447744 | bytes 2097160 | tf_op jit(solution)/shard_map/dot_general | solution.py:21
  51.3 1.8 %fusion.46 = f32[512,512]{1,0:T(8,128)S(1)} fusion(f32[512,512]{1,0:T(8,128)S(1)} %fusion.11), kind=kOutput, calls=%fused_computation.60 | convolution fusion | flops 1610612736 | bytes 2097152 | tf_op jit(solution)/shard_map/dot_general | solution.py:21
  53.1 2.9 %fusion = f32[512,512]{1,0:T(8,128)} fusion(f32[512,512]{1,0:T(8,128)S(1)} %fusion.46, f32[]{:T(128)S(6)} %div.8, f32[512,512]{1,0:T(8,128)S(1)} %get-tuple-element.6, f32[]{:T(128)S(6)} %mul_shard_map.3), kind=kOutput, calls=%fused_computation.4 | convolution fusion | flops 1612709888 | bytes 3145736 | tf_op jit(solution)/shard_map/dot_general | solution.py:21
  56.1 1.9 %fusion.7 = f32[512,512]{1,0:T(8,128)S(1)} fusion(f32[]{:T(128)S(6)} %div.8, f32[]{:T(128)S(6)} %pow.3, f32[512,512]{1,0:T(8,128)S(1)} %get-tuple-element.6, f32[]{:T(128)S(6)} %mul_shard_map.3), kind=kOutput, calls=%fused_computation.16 | convolution fusion | flops 1612972032 | bytes 2097164 | tf_op jit(solution)/shard_map/dot_general | solution.py:21
  58.0 1.8 %convolution_convert_fusion.1 = bf16[512,512]{1,0:T(8,128)(2,1)S(1)} fusion(f32[512,512]{1,0:T(8,128)S(1)} %fusion.7, f32[512,512]{1,0:T(8,128)S(1)} %copy-done.1), kind=kOutput, calls=%fused_computation.5 | convolution fusion | flops 1610874880 | bytes 2621440 | tf_op jit(solution)/shard_map/dot_general | solution.py:21
  60.1 1.8 %collective-permute-done.1 = bf16[512,512]{1,0:T(8,128)(2,1)S(1)} collective-permute-done((bf16[512,512]{1,0:T(8,128)(2,1)S(1)}, bf16[512,512]{1,0:T(8,128)(2,1)S(1)}, u32[]{:S(2)}, u32[]{:S(2)}) %collective-permute-start.1) | collective-permute-done | bytes 524320 | tf_op jit(solution)/shard_map/ppermute | solution.py:17
  61.8 0.9 %fusion.2 = bf16[1,512,256]{2,1,0:T(8,128)(2,1)S(1)} fusion(bf16[512,512]{1,0:T(8,128)(2,1)S(1)} %convolution_convert_fusion.1, bf16[512,512]{1,0:T(8,128)(2,1)S(1)} %collective-permute-done.1, pred[]{:T(512)S(6)} %eq.18, s32[]{:T(128)S(6)} %select_n.83, f32[512,256]{1,0:T(8,128)S(1)} %convert_element_type.22, f32[512,256]{1,0:T(8,128)S(1)} %bitcast_convert_fusion), kind=kOutput, calls=%fused_computation.9 | convolution fusion | flops 271581184 | bytes 2885632 | tf_op jit(solution)/shard_map/dot_general | solution.py:74
  62.8 0.4 copy.24
  63.2 0.5 broadcast.181
  63.7 2.2 %reduce = bf16[512,256]{1,0:T(8,128)(2,1)S(1)} reduce(bf16[512,1,256]{2,1,0:T(2,128)(2,1)S(1)} %bitcast.33, bf16[]{:T(256)} %broadcast.181), dimensions={1}, to_apply=%bitcast.29.reduce_sub_computation | reduce | bytes 524290
  66.0 11.8 %all_to_all.12 = bf16[4,2,16384]{2,1,0:T(2,128)(2,1)S(1)} all-to-all(bf16[4,2,16384]{2,1,0:T(2,128)(2,1)S(1)} %reshape.58), channel_id=1, replica_groups=mesh['rep'=2,'dp'=4,'mp'=2,'sub'=2] {'dp'}, dimensions={0} | all-to-all | bytes 524288 | tf_op jit(solution)/shard_map/all_to_all | solution.py:76
  78.1 0.7 copy.22
  (13 shorter events, 0.8 us)
Async XLA Ops:
  6.5 4.0 %copy-start = (bf16[256,1,256]{2,0,1:T(8,128)(2,1)S(1)}, bf16[256,1,256]{2,0,1:T(8,128)(2,1)}, u32[]{:S(2)}) copy-start(bf16[256,1,256]{2,0,1:T(8,128)(2,1)} %param.4) | copy-start | bytes 393220
  6.5 35.6 %reduce-scatter.2.cloned.1.call-start = ((), (), s32[]{:S(2)}) async-start(), calls=%async_computation.2 | async-start | bytes 1310720 | tf_op jit(solution)/shard_map/reduce_scatter | solution.py:49
  42.2 1.7 %collective-permute-start = (bf16[512,256]{1,0:T(8,128)(2,1)}, bf16[512,256]{1,0:T(8,128)(2,1)S(1)}, u32[]{:S(2)}, u32[]{:S(2)}) collective-permute-start(bf16[512,256]{1,0:T(8,128)(2,1)} %bitcast.34), channel_id=1, source_target_pairs={{0,1},{1,0},{2,3},{3,2},{4,5},{5,4},{6,7},{7,6},{8,9},{9,8},{10,11... | collective-permute-start | bytes 786440 | tf_op jit(solution)/shard_map/ppermute | solution.py:17
  56.1 1.9 %copy-start.1 = (f32[512,512]{1,0:T(8,128)S(1)}, f32[512,512]{1,0:T(8,128)}, u32[]{:S(2)}) copy-start(f32[512,512]{1,0:T(8,128)} %fusion) | copy-start | bytes 3145732
  59.9 2.0 %collective-permute-start.1 = (bf16[512,512]{1,0:T(8,128)(2,1)S(1)}, bf16[512,512]{1,0:T(8,128)(2,1)S(1)}, u32[]{:S(2)}, u32[]{:S(2)}) collective-permute-start(bf16[512,512]{1,0:T(8,128)(2,1)S(1)} %convolution_convert_fusion.1), channel_id=1, source_target_pairs={{0,1},{1,0},{2,3},{3,2},{4,5},{5,4},{6,7},{7,6},{8,9},{9,8},{10,11... | collective-permute-start | bytes 1572872 | tf_op jit(solution)/shard_map/ppermute | solution.py:17
Sparse Core Ops, SparseCore 0:
  12.3 29.8 reduce-scatter.1
where the time goes:
time: 85.9 us; the launch traced here: 85.7 us
  waiting for transfers between devices  32.5 us (38%)
  matrix products  15.6 us (18%)
  between operations  14.9 us (17%)
  blocking collectives  11.8 us (14%)
  other arithmetic  5.63 us (7%)
  local copies, waits for them, and re-layouts  4.96 us (6%)
    reduce_scatter x1, waiting for transfers between devices, shards(): lax.psum_scatter(jnp.einsum('tkb,tkh->kbh', act_sel, cot_sel, preferred_e...  30 us
    dot_general x6, matrix products, matmul_high(): return jnp.dot(left_mat, right_mat, precision=lax.Precision.HIGHEST)  13 us
    all_to_all x1, blocking collectives, shards(): lax.all_to_all(block_update[None], 'dp', split_axis=1, concat_axis=0, til...  11.8 us
    unnamed x9, local copies, waits for them, and re-layouts  3.07 us
    ppermute x2, waiting for transfers between devices, from_partner(): lax.ppermute(x, axis, [(i, i ^ 1 << distance) for i in range(lax.axis_siz...  2.53 us
    unnamed x1, other arithmetic  2.21 us
  transfers between devices with their start and end apart: 3, of which 3 were waited for; matrix products, arithmetic and copies ran while one was open for 1% of the time, Pallas kernels for 0%

commit v1 on v0

v1 whole, which is shorter than its diff:
```python
import functools
import math

import jax
import jax.numpy as jnp
from jax import lax
from jax.experimental import pallas as pl
from jax.experimental.pallas import tpu as pltpu
from jax.sharding import PartitionSpec as P

B = 512
CHUNKS = 2
DAMPING = 0.05
MESH = pl.DeviceIdType.MESH
F32 = jnp.float32
BF16 = jnp.bfloat16


def kernel(
    dp, col_count, table, act_hbm, cot_hbm, out,
    act, cot, to_right, to_left, from_left, from_right, grad, own, peer, kmat, carried, update,
    load_sem, right_send, left_send, left_recv, right_recv, sub_send, sub_recv, out_send, out_recv,
):
    z = lax.axis_index("dp")
    s = lax.axis_index("sub")
    half = own.shape[1]
    rows = B // CHUNKS
    total = dp * CHUNKS
    out_rows = B // dp

    pieces = act.shape[0]
    loads = [pltpu.make_async_copy(cot_hbm, cot, load_sem.at[pieces])]
    for i in range(pieces):
        loads.append(pltpu.make_async_copy(act_hbm.at[:, pl.ds(i * rows, rows)], act.at[i], load_sem.at[i]))
    for load in loads:
        load.start()
    barrier = pltpu.get_barrier_semaphore()
    for k in range(1, dp):
        pl.semaphore_signal(barrier, inc=1, device_id={"dp": lax.rem(z + k, dp)}, device_id_type=MESH)
    pl.semaphore_signal(barrier, inc=1, device_id={"sub": 1 - s}, device_id_type=MESH)
    for load in loads:
        load.wait()
    pl.semaphore_wait(barrier, dp)

    def partial(owner, part):
        block = table[0, owner]
        return lax.dot_general(
            act[lax.div(block, col_count) * CHUNKS + part], cot[lax.rem(block, col_count)],
            (((0,), (0,)), ((), ())), preferred_element_type=F32,
        )

    def rightward(n):
        return pltpu.make_async_remote_copy(
            src_ref=to_right.at[n], dst_ref=from_left.at[n],
            send_sem=right_send.at[n], recv_sem=left_recv.at[n],
            device_id={"dp": lax.rem(z + 1, dp)}, device_id_type=MESH,
        )

    def leftward(n):
        return pltpu.make_async_remote_copy(
            src_ref=to_left.at[n], dst_ref=from_right.at[n],
            send_sem=left_send.at[n], recv_sem=right_recv.at[n],
            device_id={"dp": lax.rem(z + dp - 1, dp)}, device_id_type=MESH,
        )

    def tick(t, carry):
        n = t - z
        owner = dp - 1 - n // CHUNKS

        @pl.when((n >= 0) & (n < total) & (owner > z))
        def _():
            piece = partial(owner, n % CHUNKS)

            @pl.when(z == 0)
            def _():
                to_right[n] = piece.astype(BF16)

            @pl.when(z > 0)
            def _():
                rightward(n).wait_recv()
                to_right[n] = (piece + from_left[n].astype(F32)).astype(BF16)

            rightward(n).start()

        m = t - (dp - 1 - z)
        owner_l = m // CHUNKS

        @pl.when((m >= 0) & (m < total) & (owner_l < z))
        def _():
            piece = partial(owner_l, m % CHUNKS)

            @pl.when(z == dp - 1)
            def _():
                to_left[m] = piece.astype(BF16)

            @pl.when(z < dp - 1)
            def _():
                leftward(m).wait_recv()
                to_left[m] = (piece + from_right[m].astype(F32)).astype(BF16)

            leftward(m).start()

        return carry

    lax.fori_loop(0, total + dp - 1, tick, 0)

    def exchange(part):
        return pltpu.make_async_remote_copy(
            src_ref=own.at[pl.ds(part * rows, rows)], dst_ref=peer.at[pl.ds(part * rows, rows)],
            send_sem=sub_send.at[part], recv_sem=sub_recv.at[part],
            device_id={"sub": 1 - s}, device_id_type=MESH,
        )

    for part in range(CHUNKS):
        here = pl.ds(part * rows, rows)
        grad[here, :] = partial(z, part)

        @pl.when(z > 0)
        def _():
            n = (dp - 1 - z) * CHUNKS + part
            rightward(n).wait_recv()
            grad[here, :] += from_left[n].astype(F32)

        @pl.when(z < dp - 1)
        def _():
            n = z * CHUNKS + part
            leftward(n).wait_recv()
            grad[here, :] += from_right[n].astype(F32)

        own[here, :] = grad[here, :].astype(BF16)
        exchange(part).start()

    nt = (((1,), (1,)), ((), ()))
    mine = own[...]
    stat = lax.dot_general(mine, mine, nt, preferred_element_type=F32)
    for part in range(CHUNKS):
        exchange(part).wait()
    theirs = peer[...]
    stat = stat + lax.dot_general(theirs, theirs, nt, preferred_element_type=F32)
    diagonal = lax.broadcasted_iota(jnp.int32, (B, B), 0) == lax.broadcasted_iota(jnp.int32, (B, B), 1)

    def total_of(x):
        return jnp.sum(jnp.sum(x, axis=0, keepdims=True), axis=1, keepdims=True)

    trace = total_of(jnp.where(diagonal, stat, 0.0))
    shift = DAMPING / B * trace
    damped = stat + jnp.where(diagonal, shift, 0.0)
    z_scale = 2.5 / jnp.sqrt(total_of(damped * damped))
    x = z_scale * damped
    xb = x.astype(BF16)
    x2 = jnp.dot(xb, xb, preferred_element_type=F32)
    d2 = 0.0625 * (10.0 * x - x2)
    fx = 0.25 * (5.0 * x - x2)
    d2b = d2.astype(BF16)
    d4 = 3.125 * d2 - jnp.dot(d2b, d2b, preferred_element_type=F32)
    w = jnp.dot(d4.astype(BF16), fx.astype(BF16), preferred_element_type=F32)
    kmat[...] = (0.3125 * x + 0.6103515625 * fx - 0.25 * w).astype(BF16)
    carried[...] = 1.5625 * grad[...] - jnp.dot(kmat[...], mine, preferred_element_type=F32)
    carried_b = carried[...].astype(BF16)
    gain = math.sqrt(B) * jnp.sqrt(z_scale)

    def deliver(k):
        there = lax.rem(z + k, dp)
        return pltpu.make_async_remote_copy(
            src_ref=update.at[there], dst_ref=out.at[z],
            send_sem=out_send.at[k - 1], recv_sem=out_recv.at[k - 1],
            device_id={"dp": there}, device_id_type=MESH,
        )

    def update_rows(there):
        at = pl.ds(pl.multiple_of(there * out_rows, out_rows), out_rows)
        product = jnp.dot(kmat[at, :], carried_b, preferred_element_type=F32)
        return (gain * (1.5625 * carried[at, :] - product)).astype(BF16)

    for k in range(1, dp):
        there = lax.rem(z + k, dp)
        update[there] = update_rows(there)
        deliver(k).start()
    out[z] = update_rows(z)

    for n in range(total):
        @pl.when(dp - 1 - n // CHUNKS > z)
        def _():
            rightward(n).wait_send()

        @pl.when(n // CHUNKS < z)
        def _():
            leftward(n).wait_send()
    for k in range(1, dp):
        came = lax.rem(z + dp - k, dp)
        deliver(k).wait_send()
        pltpu.make_async_remote_copy(
            src_ref=update.at[came], dst_ref=out.at[came],
            send_sem=out_send.at[k - 1], recv_sem=out_recv.at[k - 1],
            device_id={"dp": came}, device_id_type=MESH,
        ).wait_recv()


def shards(dp, activations, cotangent, owner_table):
    tokens, width = activations.shape
    col_count, half = cotangent.shape[1:]
    cot = cotangent.transpose(1, 0, 2)
    rows = B // CHUNKS
    total = dp * CHUNKS
    hbm = pl.BlockSpec(memory_space=pltpu.HBM)
    dma = pltpu.SemaphoreType.DMA
    return pl.pallas_call(
        functools.partial(kernel, dp, col_count),
        out_shape=jax.ShapeDtypeStruct((dp, B // dp, half), BF16),
        in_specs=[pl.BlockSpec(memory_space=pltpu.SMEM), hbm, hbm],
        out_specs=pl.BlockSpec(memory_space=pltpu.VMEM),
        scratch_shapes=[
            pltpu.VMEM((width // rows, tokens, rows), BF16),
            pltpu.VMEM((col_count, tokens, half), BF16),
            pltpu.VMEM((total, rows, half), BF16),
            pltpu.VMEM((total, rows, half), BF16),
            pltpu.VMEM((total, rows, half), BF16),
            pltpu.VMEM((total, rows, half), BF16),
            pltpu.VMEM((B, half), F32),
            pltpu.VMEM((B, half), BF16),
            pltpu.VMEM((B, half), BF16),
            pltpu.VMEM((B, B), BF16),
            pltpu.VMEM((B, half), F32),
            pltpu.VMEM((dp, B // dp, half), BF16),
            dma((width // rows + 1,)), dma((total,)), dma((total,)), dma((total,)), dma((total,)),
            dma((CHUNKS,)), dma((CHUNKS,)), dma((dp - 1,)), dma((dp - 1,)),
        ],
        compiler_params=pltpu.CompilerParams(
            collective_id=0, has_side_effects=True, vmem_limit_bytes=48 * 1024 * 1024
        ),
    )(owner_table, activations, cot)


def solution(mesh):
    in_specs = (P(("rep", "dp"), None), P(("rep", "dp"), "mp", "sub"), P(("rep", "mp"), None))
    out_specs = P(("rep", "mp"), "dp", "sub")
    return jax.shard_map(
        functools.partial(shards, mesh.shape["dp"]),
        mesh=mesh, in_specs=in_specs, out_specs=out_specs, check_vma=False,
    )
```

time: 85.9 us -> 39 us (0.45)
  Pallas kernels: 0 us -> 35.3 us
  waiting for transfers between devices: 32.5 us -> 0 us
  matrix products: 15.6 us -> 0 us
  between operations: 14.9 us -> 0.01 us
  blocking collectives: 11.8 us -> 0 us
  other arithmetic: 5.63 us -> 0 us
  local copies, waits for them, and re-layouts: 4.96 us -> 3.49 us
    pallas_call x0 -> x1, Pallas kernels: none -> 35.3 us  [shards(): pl.pallas_call(functools.partial(kernel, dp, col_count), out_shape=jax.Sh...]
    reduce_scatter x1 -> x0, waiting for transfers between devices: 30 us -> none  [shards(): lax.psum_scatter(jnp.einsum('tkb,tkh->kbh', act_sel, cot_sel, preferred_e...]
    dot_general x8 -> x0, matrix products: 15.6 us -> none  [the longest x6 13 us: matmul_high(): return jnp.dot(left_mat, right_mat, precision=lax.Precision.HIGHEST)]
    all_to_all x1 -> x0, blocking collectives: 11.8 us -> none  [shards(): lax.all_to_all(block_update[None], 'dp', split_axis=1, concat_axis=0, til...]
    ppermute x2 -> x0, waiting for transfers between devices: 2.53 us -> none  [from_partner(): lax.ppermute(x, axis, [(i, i ^ 1 << distance) for i in range(lax.axis_siz...]
    unnamed x1 -> x0, other arithmetic: 2.21 us -> none
    squeeze x1 -> x0, other arithmetic: 0.99 us -> none  [shards(): lax.psum_scatter(jnp.einsum('tkb,tkh->kbh', act_sel, cot_sel, preferred_e...]
    reduce_sum x1 -> x0, other arithmetic: 0.87 us -> none  [newton_root(): frob = jnp.sqrt(jnp.sum(damped * damped))]
  transfers between devices with their start and end apart: 3 -> 0, of which waited for: 3 -> 0; matrix products, arithmetic and copies ran while one was open for 1% -> 0% of each run, Pallas kernels for 0% -> 0%
where the time goes in v1:
time: 39 us; the launch traced here: 38.8 us
  Pallas kernels  35.3 us (91%)
  local copies, waits for them, and re-layouts  3.49 us (9%)
    pallas_call x1, Pallas kernels, shards(): pl.pallas_call(functools.partial(kernel, dp, col_count), out_shape=jax.Sh...  35.3 us
    unnamed x7, local copies, waits for them, and re-layouts  3.49 us

profile of v1, /device:TPU:0, one launch (start us, length us, event | category | flops | bytes accessed | tf_op | source)
XLA Modules:
  0.0 38.8 jit_solution(4882878717815400676)
XLA Ops:
  0.0 0.0 copy-start.2
  0.0 0.7 %copy-done.2 = s32[1,4]{1,0:T(1,128)S(1)} copy-done((s32[1,4]{1,0:T(1,128)S(1)}, s32[1,4]{1,0:T(1,128)}, u32[]{:S(2)}) %copy-start.2) | copy-done | bytes 40
  0.7 0.0 copy-start
  0.7 1.2 %copy-done = bf16[256,2048]{1,0:T(8,128)(2,1)S(1)} copy-done((bf16[256,2048]{1,0:T(8,128)(2,1)S(1)}, bf16[256,2048]{1,0:T(8,128)(2,1)}, u32[]{:S(2)}) %copy-start) | copy-done | bytes 1048600
  1.9 0.0 copy-start.1
  1.9 0.9 %copy-done.1 = bf16[256,1,256]{2,0,1:T(8,128)(2,1)S(1)} copy-done((bf16[256,1,256]{2,0,1:T(8,128)(2,1)S(1)}, bf16[256,1,256]{2,0,1:T(8,128)(2,1)}, u32[]{:S(2)}) %copy-start.1) | copy-done | bytes 131096
  2.8 35.3 %shard_map.37 = bf16[4,128,256]{2,1,0:T(8,128)(2,1)S(1)} custom-call(s32[1,4]{1,0:T(1,128)S(1)} %copy-done.2, bf16[256,2048]{1,0:T(8,128)(2,1)S(1)} %copy-done, bf16[1,256,256]{2,1,0:T(8,128)(2,1)S(1)} %bitcast.1), custom_call_target="tpu_custom_call" | custom-call | tf_op jit(solution)/shard_map/pallas_call | solution.py:207
  38.1 0.7 %copy.5 = bf16[4,128,256]{2,1,0:T(8,128)(2,1)} copy(bf16[4,128,256]{2,1,0:T(8,128)(2,1)S(1)} %shard_map.37) | data formatting | bytes 524288
Async XLA Ops:
  0.0 0.7 %copy-start.2 = (s32[1,4]{1,0:T(1,128)S(1)}, s32[1,4]{1,0:T(1,128)}, u32[]{:S(2)}) copy-start(s32[1,4]{1,0:T(1,128)} %table.1) | copy-start | bytes 52
  0.7 1.2 %copy-start = (bf16[256,2048]{1,0:T(8,128)(2,1)S(1)}, bf16[256,2048]{1,0:T(8,128)(2,1)}, u32[]{:S(2)}) copy-start(bf16[256,2048]{1,0:T(8,128)(2,1)} %act_hbm.1) | copy-start | bytes 3145732
  1.9 0.9 %copy-start.1 = (bf16[256,1,256]{2,0,1:T(8,128)(2,1)S(1)}, bf16[256,1,256]{2,0,1:T(8,128)(2,1)}, u32[]{:S(2)}) copy-start(bf16[256,1,256]{2,0,1:T(8,128)(2,1)} %param.4) | copy-start | bytes 393220

commit v2 on v1

v2 whole, which is shorter than its diff:
```python
import functools
import math

import jax
import jax.numpy as jnp
from jax import lax
from jax.experimental import pallas as pl
from jax.experimental.pallas import tpu as pltpu
from jax.sharding import PartitionSpec as P

B = 512
PIECES = 2
DAMPING = 0.05
MESH = pl.DeviceIdType.MESH
F32 = jnp.float32
BF16 = jnp.bfloat16


def kernel(
    dp, mp, col_count, table, act_hbm, cot_hbm, out,
    act, cot, act_in, both, grad, kmat, carried, update, landed,
    load_sem, act_send, act_recv, share_send, share_recv, cot_send, cot_recv, pair_send, pair_recv,
    swap_send, swap_recv, out_send, out_recv,
):
    z = lax.axis_index("dp")
    m = lax.axis_index("mp")
    s = lax.axis_index("sub")
    half = B // 2
    tokens = act.shape[0]
    part = tokens // mp
    mine_rows = pl.ds(pl.multiple_of(m * part, part), part)
    block_col = lax.rem(z, col_count)
    out_rows = B // dp

    def remote(src, dst, send, recv, where):
        return pltpu.make_async_remote_copy(
            src_ref=src, dst_ref=dst, send_sem=send, recv_sem=recv, device_id=where, device_id_type=MESH,
        )

    def columns(owner):
        return pl.ds(pl.multiple_of((lax.div(owner, col_count) * 2 + s) * half, half), half)

    load_act = pltpu.make_async_copy(act_hbm.at[:, columns(z)], act, load_sem.at[0])
    load_cot = pltpu.make_async_copy(cot_hbm, cot.at[z, s], load_sem.at[1])
    load_act.start()
    load_cot.start()
    barrier = pltpu.get_barrier_semaphore()
    for k in range(1, dp):
        pl.semaphore_signal(barrier, inc=1, device_id={"dp": lax.rem(z + k, dp)}, device_id_type=MESH)
    for k in range(1, mp):
        pl.semaphore_signal(barrier, inc=1, device_id={"mp": lax.rem(m + k, mp)}, device_id_type=MESH)
    pl.semaphore_signal(barrier, inc=1, device_id={"sub": 1 - s}, device_id_type=MESH)
    pl.semaphore_wait(barrier, dp + mp - 1)

    def pass_on(side, src, d, q):
        there = z + 1 if side == 0 else z - 1
        at = pl.ds(q * (tokens // PIECES), tokens // PIECES)
        return remote(
            src.at[:, at], cot.at[d, s, :, at], cot_send.at[side, d, q], cot_recv.at[d, q], {"dp": there}
        )

    def to_pair(src, d):
        return remote(src, cot.at[d, s, block_col], pair_send.at[d], pair_recv.at[d], {"sub": 1 - s})

    def pair_came(d):
        return remote(
            cot.at[d, 1 - s, block_col], cot.at[d, 1 - s, block_col], pair_send.at[d], pair_recv.at[d],
            {"sub": 1 - s},
        )

    def send_act(owner):
        return remote(
            act_hbm.at[mine_rows, columns(owner)], act_in.at[z, m],
            act_send.at[owner], act_recv.at[z], {"dp": owner},
        )

    def act_came(d):
        return remote(act_in.at[d, m], act_in.at[d, m], act_send.at[d], act_recv.at[d], {"dp": d})

    def share(d, k):
        there = lax.rem(m + k, mp)
        return remote(
            act_in.at[d, m], act_in.at[d, m], share_send.at[d, k - 1], share_recv.at[d, k - 1], {"mp": there},
        )

    def share_came(d, k):
        came = lax.rem(m + mp - k, mp)
        return remote(
            act_in.at[d, came], act_in.at[d, came], share_send.at[d, k - 1], share_recv.at[d, k - 1],
            {"mp": came},
        )

    has_next = (z < dp - 1, z > 0)

    def each(k, body):
        for side in range(2):
            d = z - k if side == 0 else z + k

            @pl.when((d >= 0) & (d < dp))
            def _():
                body(side, d)

    for side in range(2):
        @pl.when(has_next[side])
        def _():
            for q in range(PIECES):
                pass_on(side, cot_hbm, z, q).start()
    to_pair(cot_hbm.at[block_col], z).start()
    for k in range(1, dp):
        each(k, lambda side, d: send_act(d).start())

    def add(lhs, d, first):
        for h in range(2):
            piece = lax.dot_general(
                lhs, cot[d, h, block_col], (((0,), (0,)), ((), ())), preferred_element_type=F32
            )
            if first:
                grad[h] = piece
            else:
                grad[h] += piece

    load_act.wait()
    load_cot.wait()
    pair_came(z).wait_recv()
    add(act[...], z, True)

    def cot_arrival(side, d):
        for q in range(PIECES):
            pass_on(side, cot.at[d, s], d, q).wait_recv()

            @pl.when(has_next[side])
            def _():
                pass_on(side, cot.at[d, s], d, q).start()

        to_pair(cot.at[d, s, block_col], d).start()

    def act_arrival(side, d):
        act_came(d).wait_recv()
        for k in range(1, mp):
            share(d, k).start()

    def accumulate(side, d):
        for k in range(1, mp):
            share_came(d, k).wait_recv()
        pair_came(d).wait_recv()
        add(act_in[d].reshape(tokens, half), d, False)

    each(1, cot_arrival)
    each(1, act_arrival)
    for k in range(2, dp):
        each(k, act_arrival)
        each(k, cot_arrival)
        each(k - 1, accumulate)
    each(dp - 1, accumulate)

    for h in range(2):
        both[s, :, pl.ds(h * half, half)] = grad[h].astype(BF16)
    swap = remote(both.at[s], both.at[s], swap_send, swap_recv, {"sub": 1 - s})
    swap.start()
    swap.wait_send()
    remote(both.at[1 - s], both.at[1 - s], swap_send, swap_recv, {"sub": 1 - s}).wait_recv()

    nt = (((1,), (1,)), ((), ()))
    whole = both[...].reshape(B, B)
    stat = lax.dot_general(whole, whole, nt, preferred_element_type=F32)
    mine = both[:, :, pl.ds(pl.multiple_of(s * half, half), half)].reshape(B, half)
    diagonal = lax.broadcasted_iota(jnp.int32, (B, B), 0) == lax.broadcasted_iota(jnp.int32, (B, B), 1)

    def total_of(x):
        return jnp.sum(jnp.sum(x, axis=0, keepdims=True), axis=1, keepdims=True)

    trace = total_of(jnp.where(diagonal, stat, 0.0))
    shift = DAMPING / B * trace
    damped = stat + jnp.where(diagonal, shift, 0.0)
    z_scale = 2.5 / jnp.sqrt(total_of(damped * damped))
    x = z_scale * damped
    xb = x.astype(BF16)
    x2 = jnp.dot(xb, xb, preferred_element_type=F32)
    d2 = 0.0625 * (10.0 * x - x2)
    fx = 0.25 * (5.0 * x - x2)
    d2b = d2.astype(BF16)
    d4 = 3.125 * d2 - jnp.dot(d2b, d2b, preferred_element_type=F32)
    w = jnp.dot(d4.astype(BF16), fx.astype(BF16), preferred_element_type=F32)
    kmat[...] = (0.3125 * x + 0.6103515625 * fx - 0.25 * w).astype(BF16)
    carried[...] = 1.5625 * mine.astype(F32) - jnp.dot(kmat[...], mine, preferred_element_type=F32)
    carried_b = carried[...].astype(BF16)
    gain = math.sqrt(B) * jnp.sqrt(z_scale)

    def deliver(k):
        there = lax.rem(z + k, dp)
        return remote(
            update.at[there], landed.at[z], out_send.at[k - 1], out_recv.at[k - 1], {"dp": there}
        )

    def delivered(k):
        came = lax.rem(z + dp - k, dp)
        return remote(
            update.at[came], landed.at[came], out_send.at[k - 1], out_recv.at[k - 1], {"dp": came}
        )

    def update_rows(there):
        at = pl.ds(pl.multiple_of(there * out_rows, out_rows), out_rows)
        product = jnp.dot(kmat[at, :], carried_b, preferred_element_type=F32)
        return (gain * (1.5625 * carried[at, :] - product)).astype(BF16)

    for k in range(1, dp):
        there = lax.rem(z + k, dp)
        update[there] = update_rows(there)
        deliver(k).start()
    landed[z] = update_rows(z)

    def sent(side, d):
        send_act(d).wait_send()
        to_pair(cot.at[d, s, block_col], d).wait_send()
        for k in range(1, mp):
            share(d, k).wait_send()

        @pl.when(has_next[side])
        def _():
            for q in range(PIECES):
                pass_on(side, cot.at[d, s], d, q).wait_send()

    to_pair(cot_hbm.at[block_col], z).wait_send()
    for side in range(2):
        @pl.when(has_next[side])
        def _():
            for q in range(PIECES):
                pass_on(side, cot_hbm, z, q).wait_send()
    for k in range(1, dp):
        each(k, sent)
    for k in range(1, dp):
        deliver(k).wait_send()
        delivered(k).wait_recv()
    for slot in range(dp):
        out[slot] = landed[table[0, slot]]


def shards(dp, mp, activations, cotangent, owner_table):
    tokens = activations.shape[0]
    col_count, half = cotangent.shape[1:]
    cot = cotangent.transpose(1, 0, 2)
    hbm = pl.BlockSpec(memory_space=pltpu.HBM)
    dma = pltpu.SemaphoreType.DMA
    return pl.pallas_call(
        functools.partial(kernel, dp, mp, col_count),
        out_shape=jax.ShapeDtypeStruct((dp, B // dp, half), BF16),
        in_specs=[pl.BlockSpec(memory_space=pltpu.SMEM), hbm, hbm],
        out_specs=pl.BlockSpec(memory_space=pltpu.VMEM),
        scratch_shapes=[
            pltpu.VMEM((tokens, half), BF16),
            pltpu.VMEM((dp, 2, col_count, tokens, half), BF16),
            pltpu.VMEM((dp, mp, tokens // mp, half), BF16),
            pltpu.VMEM((2, half, B), BF16),
            pltpu.VMEM((2, half, half), F32),
            pltpu.VMEM((B, B), BF16),
            pltpu.VMEM((B, half), F32),
            pltpu.VMEM((dp, B // dp, half), BF16),
            pltpu.VMEM((dp, B // dp, half), BF16),
            dma((2,)), dma((dp,)), dma((dp,)), dma((dp, mp - 1)), dma((dp, mp - 1)), dma((2, dp, PIECES)), dma((dp, PIECES)),
            dma((dp,)), dma((dp,)), dma, dma, dma((dp - 1,)), dma((dp - 1,)),
        ],
        compiler_params=pltpu.CompilerParams(
            collective_id=0, has_side_effects=True, vmem_limit_bytes=60 * 1024 * 1024
        ),
    )(owner_table, activations, cot)


def solution(mesh):
    in_specs = (P(("rep", "dp"), None), P(("rep", "dp"), "mp", "sub"), P(("rep", "mp"), None))
    out_specs = P(("rep", "mp"), "dp", "sub")
    return jax.shard_map(
        functools.partial(shards, mesh.shape["dp"], mesh.shape["mp"]),
        mesh=mesh, in_specs=in_specs, out_specs=out_specs, check_vma=False,
    )
```

time: 39 us -> 34.4 us (0.88)
  Pallas kernels: 35.3 us -> 32.6 us
  local copies, waits for them, and re-layouts: 3.49 us -> 1.67 us
    pallas_call x1, Pallas kernels: 35.3 us -> 32.6 us  [shards(): pl.pallas_call(functools.partial(kernel, dp, mp, col_count), out_shape=ja...]
    unnamed x7 -> x1, local copies, waits for them, and re-layouts: 3.49 us -> 1.67 us
where the time goes in v2:
time: 34.4 us; the launch traced here: 34.2 us
  Pallas kernels  32.6 us (95%)
  local copies, waits for them, and re-layouts  1.67 us (5%)
    pallas_call x1, Pallas kernels, shards(): pl.pallas_call(functools.partial(kernel, dp, mp, col_count), out_shape=ja...  32.6 us
    unnamed x1, local copies, waits for them, and re-layouts  1.67 us

profile of v2, /device:TPU:0, one launch (start us, length us, event | category | flops | bytes accessed | tf_op | source)
XLA Modules:
  0.0 34.2 jit_solution(6183889210123350979)
XLA Ops:
  0.0 32.6 %shard_map.37 = bf16[4,128,256]{2,1,0:T(8,128)(2,1)} custom-call(s32[1,4]{1,0:T(1,128)} %table.1, bf16[256,2048]{1,0:T(8,128)(2,1)} %act_hbm.1, bf16[1,256,256]{2,1,0:T(8,128)(2,1)} %bitcast.1), custom_call_target="tpu_custom_call" | custom-call | tf_op jit(solution)/shard_map/pallas_call | solution.py:244
  32.6 1.7 %copy.5 = bf16[4,128,256]{2,1,0:T(8,128)(2,1)} copy(bf16[4,128,256]{2,1,0:T(8,128)(2,1)} %shard_map.37) | data formatting | bytes 524288

commit v3 on v2

--- a/solution.py
+++ b/solution.py
@@ -157,7 +157,6 @@
         both[s, :, pl.ds(h * half, half)] = grad[h].astype(BF16)
     swap = remote(both.at[s], both.at[s], swap_send, swap_recv, {"sub": 1 - s})
     swap.start()
-    swap.wait_send()
     remote(both.at[1 - s], both.at[1 - s], swap_send, swap_recv, {"sub": 1 - s}).wait_recv()
 
     nt = (((1,), (1,)), ((), ()))
@@ -203,7 +202,7 @@
         product = jnp.dot(kmat[at, :], carried_b, preferred_element_type=F32)
         return (gain * (1.5625 * carried[at, :] - product)).astype(BF16)
 
-    for k in range(1, dp):
+    for k in sorted(range(1, dp), key=lambda k: min(k, dp - k)):
         there = lax.rem(z + k, dp)
         update[there] = update_rows(there)
         deliver(k).start()
@@ -220,6 +219,7 @@
             for q in range(PIECES):
                 pass_on(side, cot.at[d, s], d, q).wait_send()
 
+    swap.wait_send()
     to_pair(cot_hbm.at[block_col], z).wait_send()
     for side in range(2):
         @pl.when(has_next[side])

time: 34.4 us -> 34.4 us (level)
  no operation moved by 1% of the time
where the time goes in v3:
time: 34.4 us; the launch traced here: 34.2 us
  Pallas kernels  32.5 us (94%)
  local copies, waits for them, and re-layouts  1.67 us (5%)
    pallas_call x1, Pallas kernels, shards(): pl.pallas_call(functools.partial(kernel, dp, mp, col_count), out_shape=ja...  32.5 us
    unnamed x1, local copies, waits for them, and re-layouts  1.67 us

profile of v3, /device:TPU:0, one launch (start us, length us, event | category | flops | bytes accessed | tf_op | source)
XLA Modules:
  0.0 34.2 jit_solution(7115043271748694037)
XLA Ops:
  0.0 32.5 %shard_map.37 = bf16[4,128,256]{2,1,0:T(8,128)(2,1)} custom-call(s32[1,4]{1,0:T(1,128)} %table.1, bf16[256,2048]{1,0:T(8,128)(2,1)} %act_hbm.1, bf16[1,256,256]{2,1,0:T(8,128)(2,1)} %bitcast.1), custom_call_target="tpu_custom_call" | custom-call | tf_op jit(solution)/shard_map/pallas_call | solution.py:244
  32.6 1.7 %copy.5 = bf16[4,128,256]{2,1,0:T(8,128)(2,1)} copy(bf16[4,128,256]{2,1,0:T(8,128)(2,1)} %shard_map.37) | data formatting | bytes 524288
